TPU v7x, 128 devices: a whole 4x4x4 slice. The times are simulated.
128 devices in a mesh: group: 8 (over z, core), local: 16 (over y, x).
Axes of the slice: x: 4, y: 4, z: 4, core: 2. Of those that a mesh axis runs over, the one named last changes fastest.
Arguments:
- tokens: bfloat16 [512, 7168], P('local'), may hold values from -6 to 6
- cotangent: bfloat16 [512, 7168], P('local'), may hold values from -6 to 6
- gate_logits: float32 [512, 24], P('local'), may hold values from -8 to 8
- route_slot: int32 [512, 8], P('local'), may hold values from 0 to 31, all different within a row; in each aligned block of 32 rows (0 to 31, 32 to 63, ...) at most 16 rows name the same one
- slot_expert: int32 [32], replicated, may hold values from 0 to 23, as said below
- w_gate: bfloat16 [32, 7168, 1024], P('local', None, 'group')
- w_up: bfloat16 [32, 7168, 1024], P('local', None, 'group')
- w_down: bfloat16 [32, 1024, 7168], P('local', 'group'), as said below
Outputs:
- mixed: bfloat16 [512, 7168], P('local', 'group')
- grad_tokens: bfloat16 [512, 7168], P('local', 'group')
- grad_logits: float32 [512, 24], P('local')
- grad_gate: bfloat16 [32, 7168, 1024], P('local', None, 'group')
- grad_up: bfloat16 [32, 7168, 1024], P('local', None, 'group')
- grad_down: bfloat16 [32, 1024, 7168], P('local', 'group')
Inputs may be any that keep to these rules, and one draw needn't show every extreme that they name: `route_slot`: each token names 8 different slots. Of the 32 tokens of one index of local, at most 16 name one slot, a bound that some block reaches of them. `slot_expert`: the even slots hold 16 different experts, the odd slots the remaining ones, each on two odd slots: slot 2i + 1 and slot 2j + 1 hold the same expert where j = i plus or minus half the size of local (the one that stays in range). Every expert is held. `w_down`: two odd slots that hold the same expert have equal weights; entries have standard deviation 1024 ** -0.5.
All inputs are finite; a program needn't handle non-finite values.
Results may differ from a plain program's by a relative error of at most 0.019.
Values may be sent and summed in bfloat16 or wider, within the bound.
No kernel may reach another device: no remote copies, remote signals or barrier semaphores. Data moves between devices by JAX's collectives and lax.ppermute only.
A program may use at most 192 MiB of HBM per device.

v0:
```python
import jax
import jax.numpy as jnp
from jax import lax
from jax.sharding import PartitionSpec as P

ROUTE_SCALE = 2.5
CONTRACT_ONE = (((1,), (1,)), ((), ()))
CONTRACT_ZERO = (((0,), (0,)), ((), ()))


def swapped(block, axis, apart):
    count = lax.axis_size(axis)
    route = []
    for low in range(count):
        high = low | 1 << apart
        if high != low and high < count:
            route += [(low, high), (high, low)]
    return lax.ppermute(block, axis, route)


def gate_weights(logits, expert_ids, experts):
    match = expert_ids[:, :, None] == jnp.arange(experts, dtype=jnp.int32)[None, None, :]
    picked = jnp.sum(jnp.where(match, logits[:, None, :], 0.0), axis=2)
    sig = jax.nn.sigmoid(picked)
    return ROUTE_SCALE * sig / jnp.sum(sig, axis=1, keepdims=True)


def activations(rows_x, rows_g, w_g, w_u, w_d):
    first = jnp.dot(rows_x, w_g, preferred_element_type=jnp.float32)
    second = jnp.dot(rows_x, w_u, preferred_element_type=jnp.float32)
    sig = jax.nn.sigmoid(first)
    silu = first * sig
    hidden = (silu * second).astype(jnp.bfloat16)
    back = lax.dot_general(rows_g, w_d, CONTRACT_ONE, preferred_element_type=jnp.float32)
    d_first = (back * second * sig * (1.0 + first * (1.0 - sig))).astype(jnp.bfloat16)
    d_second = (back * silu).astype(jnp.bfloat16)
    return (hidden, d_first, d_second)


def weight_grads(rows_x, rows_g, hidden, d_first, d_second):
    own_gate = lax.dot_general(rows_x, d_first, CONTRACT_ZERO, preferred_element_type=jnp.float32)
    own_up = lax.dot_general(rows_x, d_second, CONTRACT_ZERO, preferred_element_type=jnp.float32)
    own_down = lax.dot_general(hidden, rows_g, CONTRACT_ZERO, preferred_element_type=jnp.float32)
    return (
        own_gate.astype(jnp.bfloat16),
        own_up.astype(jnp.bfloat16),
        own_down.astype(jnp.bfloat16),
    )


def slot_pass(rows_x, rows_g, w_g, w_u, w_d):
    hidden, d_first, d_second = activations(rows_x, rows_g, w_g, w_u, w_d)
    out_rows = jnp.dot(hidden, w_d, preferred_element_type=jnp.float32).astype(jnp.bfloat16)
    both = lax.dot_general(d_first, w_g, CONTRACT_ONE, preferred_element_type=jnp.float32)
    both = both + lax.dot_general(d_second, w_u, CONTRACT_ONE, preferred_element_type=jnp.float32)
    grad_rows = both.astype(jnp.bfloat16)
    return (out_rows, grad_rows, weight_grads(rows_x, rows_g, hidden, d_first, d_second))


def per_device(tokens, cotangent, gate_logits, route_slot, slot_expert, w_gate, w_up, w_down):
    tok = tokens.shape[0]
    width = tokens.shape[1]
    top = route_slot.shape[1]
    slots = slot_expert.shape[0]
    experts = gate_logits.shape[1]
    lines = lax.axis_size("local")
    cap = top * tok // lines
    match_slot = route_slot[:, :, None] == jnp.arange(slots, dtype=jnp.int32)[None, None, :]
    expert_ids = jnp.sum(jnp.where(match_slot, slot_expert[None, None, :], 0), axis=2)
    weights, pull_back = jax.vjp(lambda lg: gate_weights(lg, expert_ids, experts), gate_logits)
    scaled = (weights[:, :, None] * cotangent.astype(jnp.float32)[:, None, :]).astype(jnp.bfloat16)
    flat = route_slot.reshape(-1)
    onehot = (flat[:, None] == jnp.arange(slots, dtype=jnp.int32)[None, :]).astype(jnp.int32)
    rank = jnp.sum((jnp.cumsum(onehot, axis=0) - onehot) * onehot, axis=1)
    target = flat * cap + rank
    placer = (jnp.arange(slots * cap, dtype=jnp.int32)[:, None] == target[None, :]).astype(
        jnp.bfloat16
    )
    token_placer = jnp.sum(placer.reshape(slots * cap, tok, top), axis=2)
    x_buffer = jnp.dot(token_placer, tokens, preferred_element_type=jnp.float32).astype(
        jnp.bfloat16
    )
    g_buffer = jnp.dot(
        placer, scaled.reshape(tok * top, width), preferred_element_type=jnp.float32
    ).astype(jnp.bfloat16)
    x_buffer = x_buffer.reshape(lines, 2 * cap, width)
    g_buffer = g_buffer.reshape(lines, 2 * cap, width)
    got_x, got_g = (
        lax.all_to_all(x_buffer, "local", split_axis=0, concat_axis=0, tiled=True),
        lax.all_to_all(g_buffer, "local", split_axis=0, concat_axis=0, tiled=True),
    )
    got_x = got_x.reshape(lines, 2, cap, width)
    got_g = got_g.reshape(lines, 2, cap, width)
    rows_cold_x = got_x[:, 0].reshape(lines * cap, width)
    rows_cold_g = got_g[:, 0].reshape(lines * cap, width)
    rows_hot_x = got_x[:, 1].reshape(lines * cap, width)
    rows_hot_g = got_g[:, 1].reshape(lines * cap, width)
    out_cold, dx_cold, grads_cold = slot_pass(
        rows_cold_x, rows_cold_g, w_gate[0], w_up[0], w_down[0]
    )
    out_hot, dx_hot, grads_hot = slot_pass(rows_hot_x, rows_hot_g, w_gate[1], w_up[1], w_down[1])
    outs_back = jnp.stack(
        [out_cold.reshape(lines, cap, width), out_hot.reshape(lines, cap, width)], axis=1
    )
    dxs_back = jnp.stack(
        [dx_cold.reshape(lines, cap, width), dx_hot.reshape(lines, cap, width)], axis=1
    )
    outs_back = outs_back.reshape(lines, 2 * cap, width)
    dxs_back = dxs_back.reshape(lines, 2 * cap, width)
    home_out, home_dx = (
        lax.all_to_all(outs_back, "local", split_axis=0, concat_axis=0, tiled=True),
        lax.all_to_all(dxs_back, "local", split_axis=0, concat_axis=0, tiled=True),
    )
    home_out = home_out.reshape(slots * cap, width)
    home_dx = home_dx.reshape(slots * cap, width)
    gathered = lax.dot_general(placer, home_out, CONTRACT_ZERO, preferred_element_type=jnp.float32)
    gathered = gathered.reshape(tok, top, width)
    partial_out = jnp.sum(weights[:, :, None] * gathered, axis=1)
    partial_dx = lax.dot_general(
        token_placer, home_dx, CONTRACT_ZERO, preferred_element_type=jnp.float32
    )
    partial_dots = jnp.sum(cotangent.astype(jnp.float32)[:, None, :] * gathered, axis=2)
    mixed, grad_tokens = (
        lax.psum_scatter(
            partial_out.astype(jnp.bfloat16), "group", scatter_dimension=1, tiled=True
        ).astype(jnp.float32),
        lax.psum_scatter(
            partial_dx.astype(jnp.bfloat16), "group", scatter_dimension=1, tiled=True
        ).astype(jnp.float32),
    )
    gate_dots = lax.psum(partial_dots, "group")
    grad_logits = pull_back(gate_dots)[0]
    partner_bit = lax.axis_size("local").bit_length() - 2
    other = swapped((grads_hot[0], grads_hot[1], grads_hot[2]), "local", partner_bit)
    joined = [
        (mine.astype(jnp.float32) + theirs.astype(jnp.float32)).astype(jnp.bfloat16)
        for mine, theirs in zip(grads_hot, other)
    ]
    grad_gate = jnp.stack([grads_cold[0], joined[0]], axis=0)
    grad_up = jnp.stack([grads_cold[1], joined[1]], axis=0)
    grad_down = jnp.stack([grads_cold[2], joined[2]], axis=0)
    return (
        mixed.astype(jnp.bfloat16),
        grad_tokens.astype(jnp.bfloat16),
        grad_logits,
        grad_gate,
        grad_up,
        grad_down,
    )


def solution(mesh):
    return jax.shard_map(
        per_device,
        mesh=mesh,
        in_specs=(
            P("local", None),
            P("local", None),
            P("local", None),
            P("local", None),
            P(),
            P("local", None, "group"),
            P("local", None, "group"),
            P("local", "group", None),
        ),
        out_specs=(
            P("local", "group"),
            P("local", "group"),
            P("local", None),
            P("local", None, "group"),
            P("local", None, "group"),
            P("local", "group", None),
        ),
        check_vma=False,
    )
```

profile of v0, /device:TPU:0, one launch (start us, length us, event | category | flops | bytes accessed | tf_op | source)
XLA Modules:
  0.0 620.1 jit_solution(16297483419287537097)
XLA Ops:
  9.5 5.0 convolution_convert_fusion.1
  14.5 7.3 %all-to-all-start = ((bf16[16,32,7168]{2,1,0:T(8,128)(2,1)}), bf16[16,32,7168]{2,1,0:T(8,128)(2,1)}, u32[]{:S(2)}, u32[]{:S(2)}) async-start(bf16[16,32,7168]{2,1,0:T(8,128)(2,1)} %bitcast.142), calls=%async_computation | async-start | bytes 14680064 | tf_op jit(solution)/shard_map/all_to_all | solution.py:89
  22.9 5.2 convolution_convert_fusion
  28.1 102.3 %all-to-all-done = bf16[16,32,7168]{2,1,0:T(8,128)(2,1)} async-done(((bf16[16,32,7168]{2,1,0:T(8,128)(2,1)}), bf16[16,32,7168]{2,1,0:T(8,128)(2,1)}, u32[]{:S(2)}, u32[]{:S(2)}) %all-to-all-start) | async-done | bytes 7340064 | tf_op jit(solution)/shard_map/all_to_all | solution.py:89
  130.5 5.8 all-to-all-start.2
  136.3 3.8 fusion.60
  141.6 3.3 copy-done.14
  148.3 94.5 %all-to-all-done.2 = bf16[16,32,7168]{2,1,0:T(8,128)(2,1)} async-done(((bf16[16,32,7168]{2,1,0:T(8,128)(2,1)}), bf16[16,32,7168]{2,1,0:T(8,128)(2,1)}, u32[]{:S(2)}, u32[]{:S(2)}) %all-to-all-start.2) | async-done | bytes 7340064 | tf_op jit(solution)/shard_map/all_to_all | solution.py:90
  242.8 3.8 fusion.59
  248.1 3.3 copy-done.15
  258.0 3.8 pad_maximum_fusion.1
  261.8 4.9 all-to-all-start.3
  266.7 4.2 convolution_convert_fusion.4
  270.9 3.4 collective-permute-start.2
  274.2 2.5 fusion.3
  285.6 3.4 collective-permute-start
  291.2 3.7 pad_maximum_fusion
  294.9 77.8 %all-to-all-done.3 = bf16[16,32,7168]{2,1,0:T(8,128)(2,1)} async-done(((bf16[16,32,7168]{2,1,0:T(8,128)(2,1)}), bf16[16,32,7168]{2,1,0:T(8,128)(2,1)}, u32[]{:S(2)}, u32[]{:S(2)}) %all-to-all-start.3) | async-done | bytes 7340064 | tf_op jit(solution)/shard_map/all_to_all | solution.py:112
  372.7 10.7 %all-to-all-start.1 = ((bf16[16,32,7168]{2,1,0:T(8,128)(2,1)}), bf16[16,32,7168]{2,1,0:T(8,128)(2,1)}, u32[]{:S(2)}, u32[]{:S(2)}) async-start(bf16[16,32,7168]{2,1,0:T(8,128)(2,1)} %bitcast.144), calls=%async_computation.1 | async-start | bytes 14680064 | tf_op jit(solution)/shard_map/all_to_all | solution.py:111
  383.8 58.0 %collective-permute-done.2 = bf16[128,7168]{1,0:T(8,128)(2,1)} collective-permute-done((bf16[128,7168]{1,0:T(8,128)(2,1)}, bf16[128,7168]{1,0:T(8,128)(2,1)}, u32[]{:S(2)}, u32[]{:S(2)}) %collective-permute-start.2) | collective-permute-done | bytes 1835040 | tf_op jit(solution)/shard_map/ppermute | solution.py:18
  441.8 2.5 fusion.11
  446.5 44.4 %collective-permute-done.1 = bf16[7168,128]{1,0:T(8,128)(2,1)} collective-permute-done((bf16[7168,128]{1,0:T(8,128)(2,1)}, bf16[7168,128]{1,0:T(8,128)(2,1)}, u32[]{:S(2)}, u32[]{:S(2)}) %collective-permute-start.1) | collective-permute-done | bytes 1835040 | tf_op jit(solution)/shard_map/ppermute | solution.py:18
  490.9 3.7 fusion.10
  494.6 35.5 %collective-permute-done = bf16[7168,128]{1,0:T(8,128)(2,1)} collective-permute-done((bf16[7168,128]{1,0:T(8,128)(2,1)S(1)}, bf16[7168,128]{1,0:T(8,128)(2,1)}, u32[]{:S(2)}, u32[]{:S(2)}) %collective-permute-start) | collective-permute-done | bytes 1835040 | tf_op jit(solution)/shard_map/ppermute | solution.py:18
  530.2 3.3 fusion.9
  533.4 4.5 convolution_convert_fusion.10
  539.8 3.7 pad_maximum_fusion.3
  543.5 4.1 all-to-all-done.1
  547.5 7.9 %multiply_reduce_fusion = (f32[32,8]{1,0:T(8,128)S(1)}, bf16[32,7168]{1,0:T(8,128)(2,1)S(1)}) fusion(f32[32,7168]{1,0:T(8,128)S(1)} %convert_element_type.121, f32[32,8]{1,0:T(8,128)S(1)} %copy.51, bf16[512,7168,1]{1,0,2:T(8,128)(2,1)} %bitcast.18, s32[256]{0:T(256)S(1)} %multiply_add_fusion.1), kind=kOutput, calls=%fused_computation.22 | convolution fusion | flops 1886289664 | bytes 8719360 | tf_op jit(solution)/shard_map/dot_general | solution.py:116
  557.4 3.7 pad_maximum_fusion.2
  561.2 14.0 %psum.7 = f32[32,8]{0,1:T(8,128)S(1)} all-reduce(f32[32,8]{0,1:T(8,128)S(1)} %copy.61), channel_id=1, replica_groups=mesh['group'=8,'local'=16] {'group'}, use_global_device_ids=true, to_apply=%region_11.12 | all-reduce | flops 256 | bytes 2048 | tf_op jit(solution)/shard_map/psum | solution.py:131
  578.8 32.8 %reduce-scatter.7.cloned.1.call-done = bf16[896,32]{1,0:T(8,128)(2,1)} async-done(((bf16[7168,32]{1,0:T(8,128)(2,1)}), bf16[896,32]{1,0:T(8,128)(2,1)}) %reduce-scatter.7.cloned.1.call-update) | async-done | bytes 57360
  (94 shorter events, 39.0 us)
Async XLA Ops:
  7.2 2.3 copy-start
  14.5 7.3 %copy-start.20 = (s32[32]{0:T(128)S(1)}, s32[32]{0:T(128)}, u32[]{:S(2)}) copy-start(s32[32]{0:T(128)} %param.12) | copy-start | bytes 388
  14.5 8.1 %copy-start.19 = (f32[32,24]{0,1:T(8,128)S(1)}, f32[32,24]{0,1:T(8,128)}, u32[]{:S(2)}) copy-start(f32[32,24]{0,1:T(8,128)} %param.10) | copy-start | bytes 9220
  14.5 8.3 %copy-start.18 = (bf16[32,7168]{1,0:T(8,128)(2,1)S(1)}, bf16[32,7168]{1,0:T(8,128)(2,1)}, u32[]{:S(2)}) copy-start(bf16[32,7168]{1,0:T(8,128)(2,1)} %param.9) | copy-start | bytes 1376260
  14.5 116.0 %all-to-all-start = ((bf16[16,32,7168]{2,1,0:T(8,128)(2,1)}), bf16[16,32,7168]{2,1,0:T(8,128)(2,1)}, u32[]{:S(2)}, u32[]{:S(2)}) async-start(bf16[16,32,7168]{2,1,0:T(8,128)(2,1)} %bitcast.142), calls=%async_computation | async-start | bytes 14680064 | tf_op jit(solution)/shard_map/all_to_all | solution.py:89
  130.5 112.4 %all-to-all-start.2 = ((bf16[16,32,7168]{2,1,0:T(8,128)(2,1)}), bf16[16,32,7168]{2,1,0:T(8,128)(2,1)}, u32[]{:S(2)}, u32[]{:S(2)}) async-start(bf16[16,32,7168]{2,1,0:T(8,128)(2,1)} %bitcast.143), calls=%async_computation.2 | async-start | bytes 14680064 | tf_op jit(solution)/shard_map/all_to_all | solution.py:90
  136.3 4.2 copy-start.12
  140.1 5.9 copy-start.4
  140.1 7.0 %copy-start.2 = (bf16[16,1,16,7168]{3,2,1,0:T(8,128)(2,1)}, bf16[16,1,16,7168]{3,2,1,0:T(8,128)(2,1)S(1)}, u32[]{:S(2)}) copy-start(bf16[16,1,16,7168]{3,2,1,0:T(8,128)(2,1)S(1)} %get-tuple-element.10) | copy-start | bytes 11010052
  140.1 4.8 copy-start.14
  242.8 4.2 copy-start.16
  246.6 5.9 copy-start.6
  246.6 5.9 copy-start.8
  246.6 4.8 copy-start.15
  253.7 2.0 copy-start.13
  261.8 111.0 %all-to-all-start.3 = ((bf16[16,32,7168]{2,1,0:T(8,128)(2,1)}), bf16[16,32,7168]{2,1,0:T(8,128)(2,1)}, u32[]{:S(2)}, u32[]{:S(2)}) async-start(bf16[16,32,7168]{2,1,0:T(8,128)(2,1)} %bitcast.145), calls=%async_computation.3 | async-start | bytes 14680064 | tf_op jit(solution)/shard_map/all_to_all | solution.py:112
  266.6 7.6 %copy-start.3 = (bf16[16,1,16,7168]{3,2,1,0:T(8,128)(2,1)S(1)}, bf16[16,1,16,7168]{3,2,1,0:T(8,128)(2,1)}, u32[]{:S(2)}) copy-start(bf16[16,1,16,7168]{3,2,1,0:T(8,128)(2,1)} %copy-done.2) | copy-start | bytes 11010052
  270.9 170.9 %collective-permute-start.2 = (bf16[128,7168]{1,0:T(8,128)(2,1)}, bf16[128,7168]{1,0:T(8,128)(2,1)}, u32[]{:S(2)}, u32[]{:S(2)}) collective-permute-start(bf16[128,7168]{1,0:T(8,128)(2,1)} %convolution_convert_fusion.4), channel_id=1, source_target_pairs={{0,8},{8,0},{1,9},{9,1},{2,10},{10,2},{3,11},{11,3},{4,12},{12,4},... | collective-permute-start | bytes 5505032 | tf_op jit(solution)/shard_map/ppermute | solution.py:18
  276.7 2.4 copy-start.5
  281.5 2.0 copy-start.7
  282.7 6.3 %copy-start.17 = (bf16[2,128,7168]{2,1,0:T(8,128)(2,1)S(1)}, bf16[2,128,7168]{2,1,0:T(8,128)(2,1)}, u32[]{:S(2)}) copy-start(bf16[2,128,7168]{2,1,0:T(8,128)(2,1)} %param.15) | copy-start | bytes 11010052
  285.5 205.4 %collective-permute-start.1 = (bf16[7168,128]{1,0:T(8,128)(2,1)}, bf16[7168,128]{1,0:T(8,128)(2,1)}, u32[]{:S(2)}, u32[]{:S(2)}) collective-permute-start(bf16[7168,128]{1,0:T(8,128)(2,1)} %convolution_convert_fusion.6), channel_id=1, source_target_pairs={{0,8},{8,0},{1,9},{9,1},{2,10},{10,2},{3,11},{11,3},{4,12},{12,4},... | collective-permute-start | bytes 5505032 | tf_op jit(solution)/shard_map/ppermute | solution.py:18
  285.6 244.5 %collective-permute-start = (bf16[7168,128]{1,0:T(8,128)(2,1)S(1)}, bf16[7168,128]{1,0:T(8,128)(2,1)}, u32[]{:S(2)}, u32[]{:S(2)}) collective-permute-start(bf16[7168,128]{1,0:T(8,128)(2,1)S(1)} %convolution_convert_fusion.8), channel_id=1, source_target_pairs={{0,8},{8,0},{1,9},{9,1},{2,10},{10,2},{3,11},{11,3},{4,12},{12,4},... | collective-permute-start | bytes 5505032 | tf_op jit(solution)/shard_map/ppermute | solution.py:18
  372.7 174.8 %all-to-all-start.1 = ((bf16[16,32,7168]{2,1,0:T(8,128)(2,1)}), bf16[16,32,7168]{2,1,0:T(8,128)(2,1)}, u32[]{:S(2)}, u32[]{:S(2)}) async-start(bf16[16,32,7168]{2,1,0:T(8,128)(2,1)} %bitcast.144), calls=%async_computation.1 | async-start | bytes 14680064 | tf_op jit(solution)/shard_map/all_to_all | solution.py:111
  383.5 193.7 %reduce-scatter.9.cloned.1.call-start = ((), (), s32[]{:S(2)}) async-start(), calls=%async_computation.7 | async-start | bytes 2064384
  383.8 60.5 %copy-start.11 = (bf16[1,128,7168]{2,1,0:T(8,128)(2,1)S(1)}, bf16[1,128,7168]{2,1,0:T(8,128)(2,1)}, u32[]{:S(2)}) copy-start(bf16[1,128,7168]{2,1,0:T(8,128)(2,1)} %fusion.4) | copy-start | bytes 5505028
  537.9 1.9 copy-start.10
  539.6 72.0 %reduce-scatter.7.cloned.1.call-start = ((), (), s32[]{:S(2)}) async-start(), calls=%async_computation.6 | async-start | bytes 2064384
  555.5 1.9 copy-start.9
  557.4 55.9 %copy-start.1 = (bf16[32,7168]{1,0:T(8,128)(2,1)S(1)}, bf16[32,7168]{1,0:T(8,128)(2,1)}, u32[]{:S(2)}) copy-start(bf16[32,7168]{1,0:T(8,128)(2,1)} %param.8) | copy-start | bytes 1376260
Sparse Core Ops, SparseCore 0:
  539.7 37.4 reduce-scatter.8
  579.6 31.9 reduce-scatter.6
where the time goes:
time: 621 us; the launch traced here: 620 us
  waiting for transfers between devices  451 us (73%)
  matrix products  50.6 us (8%)
  starting transfers between devices  36 us (6%)
  other arithmetic  29 us (5%)
  local copies, waits for them, and re-layouts  25.2 us (4%)
  between operations  14.5 us (2%)
  blocking collectives  14 us (2%)
    ppermute x3, waiting for transfers between devices, swapped(): return lax.ppermute(block, axis, route)  138 us
    all_to_all x1, waiting for transfers between devices, per_device(): lax.all_to_all(x_buffer, 'local', split_axis=0, concat_axis=0, tiled=True)  102 us
    all_to_all x1, waiting for transfers between devices, per_device(): lax.all_to_all(g_buffer, 'local', split_axis=0, concat_axis=0, tiled=True)  94.5 us
    all_to_all x1, waiting for transfers between devices, per_device(): lax.all_to_all(dxs_back, 'local', split_axis=0, concat_axis=0, tiled=True)  77.8 us
    unnamed x4, waiting for transfers between devices  34.1 us
    unnamed x47, local copies, waits for them, and re-layouts  17 us
    psum x1, blocking collectives, per_device(): gate_dots = lax.psum(partial_dots, 'group')  14 us
  transfers between devices with their start and end apart: 9, of which 9 were waited for; matrix products, arithmetic and copies ran while one was open for 12% of the time, Pallas kernels for 0%

commit v1 on v0

--- a/solution.py
+++ b/solution.py
@@ -6,6 +6,28 @@
 ROUTE_SCALE = 2.5
 CONTRACT_ONE = (((1,), (1,)), ((), ()))
 CONTRACT_ZERO = (((0,), (0,)), ((), ()))
+
+
+def split_up(x, dim, peers):
+    before, after = (x.shape[:dim], x.shape[dim + 1 :])
+    return jnp.moveaxis(x.reshape(*before, peers, -1, *after), dim, 0)
+
+
+def in_order(blocks, dim):
+    dims = list(blocks.shape[1:])
+    dims[dim] *= blocks.shape[0]
+    return jnp.moveaxis(blocks, 0, dim).reshape(dims)
+
+
+def swapped_with_each(shard, axis, split_dim, concat_dim):
+    peers, position = (lax.axis_size(axis), lax.axis_index(axis))
+    parts = split_up(shard, split_dim, peers)
+    gathered = [parts[position]]
+    for lap in range(1, peers):
+        sent = parts[position ^ lap]
+        gathered.append(lax.ppermute(sent, axis, [(i, i ^ lap) for i in range(peers)]))
+    parts = jnp.stack(gathered)[position ^ jnp.arange(peers)]
+    return in_order(parts, concat_dim)
 
 
 def swapped(block, axis, apart):
@@ -86,7 +108,7 @@
     x_buffer = x_buffer.reshape(lines, 2 * cap, width)
     g_buffer = g_buffer.reshape(lines, 2 * cap, width)
     got_x, got_g = (
-        lax.all_to_all(x_buffer, "local", split_axis=0, concat_axis=0, tiled=True),
+        swapped_with_each(x_buffer, "local", 0, 0),
         lax.all_to_all(g_buffer, "local", split_axis=0, concat_axis=0, tiled=True),
     )
     got_x = got_x.reshape(lines, 2, cap, width)

time: 621 us -> 660 us (1.063); the launches traced: 620 us -> 651 us
  starting transfers between devices: 36 us -> 179 us
  waiting for transfers between devices: 451 us -> 315 us
  local copies, waits for them, and re-layouts: 25.2 us -> 49.4 us
    ppermute x3, waiting for transfers between devices: 138 us -> 0.01 us  [swapped(): return lax.ppermute(block, axis, route)]
    ppermute x0 -> x15, waiting for transfers between devices: none -> 134 us  [swapped_with_each(): lax.ppermute(sent, axis, [(i, i ^ lap) for i in range(peers)])]
    all_to_all x1 -> x0, waiting for transfers between devices: 102 us -> none  [per_device(): lax.all_to_all(x_buffer, 'local', split_axis=0, concat_axis=0, tiled=True)]
    all_to_all x1, waiting for transfers between devices: 94.5 us -> 0.01 us  [per_device(): lax.all_to_all(g_buffer, 'local', split_axis=0, concat_axis=0, tiled=True)]
    all_to_all x1, starting transfers between devices: 10.7 us -> 95.1 us  [per_device(): lax.all_to_all(outs_back, 'local', split_axis=0, concat_axis=0, tiled=True)]
    all_to_all x1, waiting for transfers between devices: 4.05 us -> 87 us  [per_device(): lax.all_to_all(outs_back, 'local', split_axis=0, concat_axis=0, tiled=True)]
    ppermute x0 -> x15, starting transfers between devices: none -> 57.3 us  [swapped_with_each(): lax.ppermute(sent, axis, [(i, i ^ lap) for i in range(peers)])]
    unnamed x4, waiting for transfers between devices: 34.1 us -> 12.9 us
  transfers between devices with their start and end apart: 9 -> 23, of which waited for: 9 -> 6; matrix products, arithmetic and copies ran while one was open for 12% -> 14% of each run, Pallas kernels for 0% -> 0%
where the time goes in v1:
time: 660 us; the launch traced here: 651 us
  waiting for transfers between devices  315 us (48%)
  starting transfers between devices  179 us (27%)
  local copies, waits for them, and re-layouts  49.4 us (7%)
  matrix products  47.9 us (7%)
  other arithmetic  30 us (5%)
  blocking collectives  14.9 us (2%)
  between operations  14.9 us (2%)
    ppermute x15, waiting for transfers between devices, swapped_with_each(): lax.ppermute(sent, axis, [(i, i ^ lap) for i in range(peers)])  134 us
    all_to_all x1, starting transfers between devices, per_device(): lax.all_to_all(outs_back, 'local', split_axis=0, concat_axis=0, tiled=True)  95.1 us
    all_to_all x1, waiting for transfers between devices, per_device(): lax.all_to_all(outs_back, 'local', split_axis=0, concat_axis=0, tiled=True)  87 us
    all_to_all x1, waiting for transfers between devices, per_device(): lax.all_to_all(dxs_back, 'local', split_axis=0, concat_axis=0, tiled=True)  80.9 us
    ppermute x15, starting transfers between devices, swapped_with_each(): lax.ppermute(sent, axis, [(i, i ^ lap) for i in range(peers)])  57.3 us
    unnamed x73, local copies, waits for them, and re-layouts  30.2 us
    psum x1, blocking collectives, per_device(): gate_dots = lax.psum(partial_dots, 'group')  14.9 us
  transfers between devices with their start and end apart: 23, of which 6 were waited for; matrix products, arithmetic and copies ran while one was open for 14% of the time, Pallas kernels for 0%

profile of v1, /device:TPU:0, one launch (start us, length us, event | category | flops | bytes accessed | tf_op | source)
XLA Modules:
  0.0 651.3 jit_solution(8438356610027915209)
XLA Ops:
  23.4 5.2 convolution_convert_fusion
  28.7 8.0 %all-to-all-start.1 = ((bf16[16,32,7168]{2,1,0:T(8,128)(2,1)}), bf16[16,32,7168]{2,1,0:T(8,128)(2,1)}, u32[]{:S(2)}, u32[]{:S(2)}) async-start(bf16[16,32,7168]{2,1,0:T(8,128)(2,1)} %bitcast.206), calls=%async_computation.1 | async-start | bytes 14680064 | tf_op jit(solution)/shard_map/all_to_all | solution.py:112
  37.5 4.3 collective-permute-start.5
  50.3 5.4 collective-permute-done.4
  57.0 107.4 %collective-permute-done.5 = bf16[1,32,7168]{2,1,0:T(8,128)(2,1)S(1)} collective-permute-done((bf16[1,32,7168]{2,1,0:T(8,128)(2,1)}, bf16[1,32,7168]{2,1,0:T(8,128)(2,1)S(1)}, u32[]{:S(2)}, u32[]{:S(2)}) %collective-permute-start.5) | collective-permute-done | bytes 458784 | tf_op jit(solution)/shard_map/ppermute | solution.py:28
  164.4 14.5 %collective-permute-start.10 = (bf16[1,32,7168]{2,1,0:T(8,128)(2,1)S(1)}, bf16[1,32,7168]{2,1,0:T(8,128)(2,1)S(1)}, u32[]{:S(2)}, u32[]{:S(2)}) collective-permute-start(bf16[1,32,7168]{2,1,0:T(8,128)(2,1)S(1)} %copy-done.23), channel_id=1, source_target_pairs={{0,11},{1,10},{2,9},{3,8},{4,15},{5,14},{6,13},{7,12},{8,3},{9,2},... | collective-permute-start | bytes 1376264 | tf_op jit(solution)/shard_map/ppermute | solution.py:28
  180.6 8.4 %collective-permute-start.12 = (bf16[1,32,7168]{2,1,0:T(8,128)(2,1)S(1)}, bf16[1,32,7168]{2,1,0:T(8,128)(2,1)S(1)}, u32[]{:S(2)}, u32[]{:S(2)}) collective-permute-start(bf16[1,32,7168]{2,1,0:T(8,128)(2,1)S(1)} %copy-done.21), channel_id=1, source_target_pairs={{0,13},{1,12},{2,15},{3,14},{4,9},{5,8},{6,11},{7,10},{8,5},{9,4},... | collective-permute-start | bytes 1376264 | tf_op jit(solution)/shard_map/ppermute | solution.py:28
  189.9 8.9 %collective-permute-start.13 = (bf16[1,32,7168]{2,1,0:T(8,128)(2,1)S(1)}, bf16[1,32,7168]{2,1,0:T(8,128)(2,1)S(1)}, u32[]{:S(2)}, u32[]{:S(2)}) collective-permute-start(bf16[1,32,7168]{2,1,0:T(8,128)(2,1)S(1)} %copy-done.20), channel_id=1, source_target_pairs={{0,14},{1,15},{2,12},{3,13},{4,10},{5,11},{6,8},{7,9},{8,6},{9,7},... | collective-permute-start | bytes 1376264 | tf_op jit(solution)/shard_map/ppermute | solution.py:28
  199.6 9.9 %collective-permute-start.14 = (bf16[1,32,7168]{2,1,0:T(8,128)(2,1)S(1)}, bf16[1,32,7168]{2,1,0:T(8,128)(2,1)S(1)}, u32[]{:S(2)}, u32[]{:S(2)}) collective-permute-start(bf16[1,32,7168]{2,1,0:T(8,128)(2,1)S(1)} %copy-done.19), channel_id=1, source_target_pairs={{0,15},{1,14},{2,13},{3,12},{4,11},{5,10},{6,9},{7,8},{8,7},{9,6},... | collective-permute-start | bytes 1376264 | tf_op jit(solution)/shard_map/ppermute | solution.py:28
  211.2 21.2 %collective-permute-done.11 = bf16[1,32,7168]{2,1,0:T(8,128)(2,1)S(1)} collective-permute-done((bf16[1,32,7168]{2,1,0:T(8,128)(2,1)S(1)}, bf16[1,32,7168]{2,1,0:T(8,128)(2,1)S(1)}, u32[]{:S(2)}, u32[]{:S(2)}) %collective-permute-start.11) | collective-permute-done | bytes 458784 | tf_op jit(solution)/shard_map/ppermute | solution.py:28
  235.6 7.0 %gather_fusion = bf16[16,32,7168]{2,1,0:T(8,128)(2,1)} fusion(bf16[16,32,7168]{2,1,0:T(8,128)(2,1)} %bitcast.218, s32[1024]{0:T(1024)S(1)} %pad_clamp_fusion), kind=kCustom, calls=%fused_computation | custom fusion | bytes 14680128 | tf_op jit(solution)/shard_map/gather | solution.py:29
  242.6 3.8 fusion.61
  247.9 3.2 copy-done.14
  254.6 3.8 fusion.60
  259.9 3.3 copy-done.15
  270.0 3.6 pad_maximum_fusion.1
  273.5 11.9 %all-to-all-start.2 = ((bf16[16,32,7168]{2,1,0:T(8,128)(2,1)}), bf16[16,32,7168]{2,1,0:T(8,128)(2,1)}, u32[]{:S(2)}, u32[]{:S(2)}) async-start(bf16[16,32,7168]{2,1,0:T(8,128)(2,1)} %bitcast.208), calls=%async_computation.2 | async-start | bytes 14680064 | tf_op jit(solution)/shard_map/all_to_all | solution.py:134
  285.5 4.2 convolution_convert_fusion.4
  289.6 3.4 collective-permute-start.17
  304.4 3.4 collective-permute-start.15
  310.0 3.7 pad_maximum_fusion
  313.7 80.9 %all-to-all-done.2 = bf16[16,32,7168]{2,1,0:T(8,128)(2,1)} async-done(((bf16[16,32,7168]{2,1,0:T(8,128)(2,1)}), bf16[16,32,7168]{2,1,0:T(8,128)(2,1)}, u32[]{:S(2)}, u32[]{:S(2)}) %all-to-all-start.2) | async-done | bytes 7340064 | tf_op jit(solution)/shard_map/all_to_all | solution.py:134
  394.5 95.1 %all-to-all-start = ((bf16[16,32,7168]{2,1,0:T(8,128)(2,1)}), bf16[16,32,7168]{2,1,0:T(8,128)(2,1)}, u32[]{:S(2)}, u32[]{:S(2)}) async-start(bf16[16,32,7168]{2,1,0:T(8,128)(2,1)} %bitcast.207), calls=%async_computation | async-start | bytes 14680064 | tf_op jit(solution)/shard_map/all_to_all | solution.py:133
  494.7 3.8 fusion.10
  498.5 3.3 fusion.9
  501.7 4.4 convolution_convert_fusion.10
  508.1 3.7 pad_maximum_fusion.3
  511.8 87.0 %all-to-all-done = bf16[16,32,7168]{2,1,0:T(8,128)(2,1)} async-done(((bf16[16,32,7168]{2,1,0:T(8,128)(2,1)}), bf16[16,32,7168]{2,1,0:T(8,128)(2,1)}, u32[]{:S(2)}, u32[]{:S(2)}) %all-to-all-start) | async-done | bytes 7340064 | tf_op jit(solution)/shard_map/all_to_all | solution.py:133
  598.8 7.9 %multiply_reduce_fusion = (f32[32,8]{1,0:T(8,128)S(1)}, bf16[32,7168]{1,0:T(8,128)(2,1)S(1)}) fusion(f32[32,7168]{1,0:T(8,128)S(1)} %convert_element_type.121, f32[32,8]{1,0:T(8,128)S(1)} %copy.51, bf16[512,7168,1]{1,0,2:T(8,128)(2,1)} %bitcast.50, s32[256]{0:T(256)S(1)} %multiply_add_fusion.1), kind=kOutput, calls=%fused_computation.23 | convolution fusion | flops 1886289664 | bytes 8719360 | tf_op jit(solution)/shard_map/dot_general | solution.py:138
  608.6 3.7 pad_maximum_fusion.2
  612.4 14.9 %psum.7 = f32[32,8]{0,1:T(8,128)S(1)} all-reduce(f32[32,8]{0,1:T(8,128)S(1)} %copy.61), channel_id=1, replica_groups=mesh['group'=8,'local'=16] {'group'}, use_global_device_ids=true, to_apply=%region_11.12 | all-reduce | flops 256 | bytes 2048 | tf_op jit(solution)/shard_map/psum | solution.py:153
  629.6 12.9 %reduce-scatter.7.cloned.1.call-done = bf16[896,32]{1,0:T(8,128)(2,1)} async-done(((bf16[7168,32]{1,0:T(8,128)(2,1)}), bf16[896,32]{1,0:T(8,128)(2,1)}) %reduce-scatter.7.cloned.1.call-update) | async-done | bytes 57360
  (153 shorter events, 74.4 us)
Async XLA Ops:
  11.7 9.6 %copy-start.26 = (s32[32]{0:T(128)S(1)}, s32[32]{0:T(128)}, u32[]{:S(2)}) copy-start(s32[32]{0:T(128)} %param.12) | copy-start | bytes 388
  11.7 10.4 %copy-start.25 = (f32[32,24]{0,1:T(8,128)S(1)}, f32[32,24]{0,1:T(8,128)}, u32[]{:S(2)}) copy-start(f32[32,24]{0,1:T(8,128)} %param.10) | copy-start | bytes 9220
  14.8 21.9 %collective-permute-start = (bf16[1,32,7168]{2,1,0:T(8,128)(2,1)}, bf16[1,32,7168]{2,1,0:T(8,128)(2,1)S(1)}, u32[]{:S(2)}, u32[]{:S(2)}) collective-permute-start(bf16[1,32,7168]{2,1,0:T(8,128)(2,1)} %get-tuple-element.26), channel_id=1, source_target_pairs={{0,1},{1,0},{2,3},{3,2},{4,5},{5,4},{6,7},{7,6},{8,9},{9,8},{10,11... | collective-permute-start | bytes 1376264 | tf_op jit(solution)/shard_map/ppermute | solution.py:28
  16.4 27.3 %collective-permute-start.1 = (bf16[1,32,7168]{2,1,0:T(8,128)(2,1)}, bf16[1,32,7168]{2,1,0:T(8,128)(2,1)S(1)}, u32[]{:S(2)}, u32[]{:S(2)}) collective-permute-start(bf16[1,32,7168]{2,1,0:T(8,128)(2,1)} %get-tuple-element.25), channel_id=1, source_target_pairs={{0,2},{1,3},{2,0},{3,1},{4,6},{5,7},{6,4},{7,5},{8,10},{9,11},{10,... | collective-permute-start | bytes 1376264 | tf_op jit(solution)/shard_map/ppermute | solution.py:28
  19.1 26.6 %collective-permute-start.2 = (bf16[1,32,7168]{2,1,0:T(8,128)(2,1)}, bf16[1,32,7168]{2,1,0:T(8,128)(2,1)S(1)}, u32[]{:S(2)}, u32[]{:S(2)}) collective-permute-start(bf16[1,32,7168]{2,1,0:T(8,128)(2,1)} %get-tuple-element.24), channel_id=1, source_target_pairs={{0,3},{1,2},{2,1},{3,0},{4,7},{5,6},{6,5},{7,4},{8,11},{9,10},{10,... | collective-permute-start | bytes 1376264 | tf_op jit(solution)/shard_map/ppermute | solution.py:28
  19.5 30.0 %collective-permute-start.3 = (bf16[1,32,7168]{2,1,0:T(8,128)(2,1)}, bf16[1,32,7168]{2,1,0:T(8,128)(2,1)S(1)}, u32[]{:S(2)}, u32[]{:S(2)}) collective-permute-start(bf16[1,32,7168]{2,1,0:T(8,128)(2,1)} %get-tuple-element.23), channel_id=1, source_target_pairs={{0,4},{1,5},{2,6},{3,7},{4,0},{5,1},{6,2},{7,3},{8,12},{9,13},{10,... | collective-permute-start | bytes 1376264 | tf_op jit(solution)/shard_map/ppermute | solution.py:28
  21.2 34.5 %collective-permute-start.4 = (bf16[1,32,7168]{2,1,0:T(8,128)(2,1)}, bf16[1,32,7168]{2,1,0:T(8,128)(2,1)S(1)}, u32[]{:S(2)}, u32[]{:S(2)}) collective-permute-start(bf16[1,32,7168]{2,1,0:T(8,128)(2,1)} %get-tuple-element.22), channel_id=1, source_target_pairs={{0,5},{1,4},{2,7},{3,6},{4,1},{5,0},{6,3},{7,2},{8,13},{9,12},{10,... | collective-permute-start | bytes 1376264 | tf_op jit(solution)/shard_map/ppermute | solution.py:28
  28.7 225.9 %all-to-all-start.1 = ((bf16[16,32,7168]{2,1,0:T(8,128)(2,1)}), bf16[16,32,7168]{2,1,0:T(8,128)(2,1)}, u32[]{:S(2)}, u32[]{:S(2)}) async-start(bf16[16,32,7168]{2,1,0:T(8,128)(2,1)} %bitcast.206), calls=%async_computation.1 | async-start | bytes 14680064 | tf_op jit(solution)/shard_map/all_to_all | solution.py:112
  36.7 19.1 %copy-start.24 = (bf16[1,32,7168]{2,1,0:T(8,128)(2,1)S(1)}, bf16[1,32,7168]{2,1,0:T(8,128)(2,1)}, u32[]{:S(2)}) copy-start(bf16[1,32,7168]{2,1,0:T(8,128)(2,1)} %get-tuple-element.17) | copy-start | bytes 1376260
  36.7 127.7 %copy-start.23 = (bf16[1,32,7168]{2,1,0:T(8,128)(2,1)S(1)}, bf16[1,32,7168]{2,1,0:T(8,128)(2,1)}, u32[]{:S(2)}) copy-start(bf16[1,32,7168]{2,1,0:T(8,128)(2,1)} %get-tuple-element.16) | copy-start | bytes 1376260
  36.7 143.1 %copy-start.22 = (bf16[1,32,7168]{2,1,0:T(8,128)(2,1)S(1)}, bf16[1,32,7168]{2,1,0:T(8,128)(2,1)}, u32[]{:S(2)}) copy-start(bf16[1,32,7168]{2,1,0:T(8,128)(2,1)} %get-tuple-element.15) | copy-start | bytes 1376260
  36.7 143.9 %copy-start.21 = (bf16[1,32,7168]{2,1,0:T(8,128)(2,1)S(1)}, bf16[1,32,7168]{2,1,0:T(8,128)(2,1)}, u32[]{:S(2)}) copy-start(bf16[1,32,7168]{2,1,0:T(8,128)(2,1)} %get-tuple-element.14) | copy-start | bytes 1376260
  37.5 126.9 %collective-permute-start.5 = (bf16[1,32,7168]{2,1,0:T(8,128)(2,1)}, bf16[1,32,7168]{2,1,0:T(8,128)(2,1)S(1)}, u32[]{:S(2)}, u32[]{:S(2)}) collective-permute-start(bf16[1,32,7168]{2,1,0:T(8,128)(2,1)} %get-tuple-element.21), channel_id=1, source_target_pairs={{0,6},{1,7},{2,4},{3,5},{4,2},{5,3},{6,0},{7,1},{8,14},{9,15},{10,... | collective-permute-start | bytes 1376264 | tf_op jit(solution)/shard_map/ppermute | solution.py:28
  41.8 148.0 %copy-start.20 = (bf16[1,32,7168]{2,1,0:T(8,128)(2,1)S(1)}, bf16[1,32,7168]{2,1,0:T(8,128)(2,1)}, u32[]{:S(2)}) copy-start(bf16[1,32,7168]{2,1,0:T(8,128)(2,1)} %get-tuple-element.13) | copy-start | bytes 1376260
  43.7 155.9 %copy-start.19 = (bf16[1,32,7168]{2,1,0:T(8,128)(2,1)S(1)}, bf16[1,32,7168]{2,1,0:T(8,128)(2,1)}, u32[]{:S(2)}) copy-start(bf16[1,32,7168]{2,1,0:T(8,128)(2,1)} %get-tuple-element.12) | copy-start | bytes 1376260
  43.7 136.1 %collective-permute-start.6 = (bf16[1,32,7168]{2,1,0:T(8,128)(2,1)}, bf16[1,32,7168]{2,1,0:T(8,128)(2,1)S(1)}, u32[]{:S(2)}, u32[]{:S(2)}) collective-permute-start(bf16[1,32,7168]{2,1,0:T(8,128)(2,1)} %get-tuple-element.20), channel_id=1, source_target_pairs={{0,7},{1,6},{2,5},{3,4},{4,3},{5,2},{6,1},{7,0},{8,15},{9,14},{10,... | collective-permute-start | bytes 1376264 | tf_op jit(solution)/shard_map/ppermute | solution.py:28
  45.7 134.9 %collective-permute-start.7 = (bf16[1,32,7168]{2,1,0:T(8,128)(2,1)}, bf16[1,32,7168]{2,1,0:T(8,128)(2,1)S(1)}, u32[]{:S(2)}, u32[]{:S(2)}) collective-permute-start(bf16[1,32,7168]{2,1,0:T(8,128)(2,1)} %get-tuple-element.19), channel_id=1, source_target_pairs={{0,8},{1,9},{2,10},{3,11},{4,12},{5,13},{6,14},{7,15},{8,0},{9,1},... | collective-permute-start | bytes 1376264 | tf_op jit(solution)/shard_map/ppermute | solution.py:28
  49.5 140.4 %collective-permute-start.8 = (bf16[1,32,7168]{2,1,0:T(8,128)(2,1)}, bf16[1,32,7168]{2,1,0:T(8,128)(2,1)S(1)}, u32[]{:S(2)}, u32[]{:S(2)}) collective-permute-start(bf16[1,32,7168]{2,1,0:T(8,128)(2,1)} %get-tuple-element.18), channel_id=1, source_target_pairs={{0,9},{1,8},{2,11},{3,10},{4,13},{5,12},{6,15},{7,14},{8,1},{9,0},... | collective-permute-start | bytes 1376264 | tf_op jit(solution)/shard_map/ppermute | solution.py:28
  55.7 143.9 %collective-permute-start.9 = (bf16[1,32,7168]{2,1,0:T(8,128)(2,1)S(1)}, bf16[1,32,7168]{2,1,0:T(8,128)(2,1)S(1)}, u32[]{:S(2)}, u32[]{:S(2)}) collective-permute-start(bf16[1,32,7168]{2,1,0:T(8,128)(2,1)S(1)} %copy-done.24), channel_id=1, source_target_pairs={{0,10},{1,11},{2,8},{3,9},{4,14},{5,15},{6,12},{7,13},{8,2},{9,3},... | collective-permute-start | bytes 1376264 | tf_op jit(solution)/shard_map/ppermute | solution.py:28
  164.4 45.9 %collective-permute-start.10 = (bf16[1,32,7168]{2,1,0:T(8,128)(2,1)S(1)}, bf16[1,32,7168]{2,1,0:T(8,128)(2,1)S(1)}, u32[]{:S(2)}, u32[]{:S(2)}) collective-permute-start(bf16[1,32,7168]{2,1,0:T(8,128)(2,1)S(1)} %copy-done.23), channel_id=1, source_target_pairs={{0,11},{1,10},{2,9},{3,8},{4,15},{5,14},{6,13},{7,12},{8,3},{9,2},... | collective-permute-start | bytes 1376264 | tf_op jit(solution)/shard_map/ppermute | solution.py:28
  179.8 52.6 %collective-permute-start.11 = (bf16[1,32,7168]{2,1,0:T(8,128)(2,1)S(1)}, bf16[1,32,7168]{2,1,0:T(8,128)(2,1)S(1)}, u32[]{:S(2)}, u32[]{:S(2)}) collective-permute-start(bf16[1,32,7168]{2,1,0:T(8,128)(2,1)S(1)} %copy-done.22), channel_id=1, source_target_pairs={{0,12},{1,13},{2,14},{3,15},{4,8},{5,9},{6,10},{7,11},{8,4},{9,5},... | collective-permute-start | bytes 1376264 | tf_op jit(solution)/shard_map/ppermute | solution.py:28
  180.6 52.5 %collective-permute-start.12 = (bf16[1,32,7168]{2,1,0:T(8,128)(2,1)S(1)}, bf16[1,32,7168]{2,1,0:T(8,128)(2,1)S(1)}, u32[]{:S(2)}, u32[]{:S(2)}) collective-permute-start(bf16[1,32,7168]{2,1,0:T(8,128)(2,1)S(1)} %copy-done.21), channel_id=1, source_target_pairs={{0,13},{1,12},{2,15},{3,14},{4,9},{5,8},{6,11},{7,10},{8,5},{9,4},... | collective-permute-start | bytes 1376264 | tf_op jit(solution)/shard_map/ppermute | solution.py:28
  189.9 44.1 %collective-permute-start.13 = (bf16[1,32,7168]{2,1,0:T(8,128)(2,1)S(1)}, bf16[1,32,7168]{2,1,0:T(8,128)(2,1)S(1)}, u32[]{:S(2)}, u32[]{:S(2)}) collective-permute-start(bf16[1,32,7168]{2,1,0:T(8,128)(2,1)S(1)} %copy-done.20), channel_id=1, source_target_pairs={{0,14},{1,15},{2,12},{3,13},{4,10},{5,11},{6,8},{7,9},{8,6},{9,7},... | collective-permute-start | bytes 1376264 | tf_op jit(solution)/shard_map/ppermute | solution.py:28
  199.6 35.2 %collective-permute-start.14 = (bf16[1,32,7168]{2,1,0:T(8,128)(2,1)S(1)}, bf16[1,32,7168]{2,1,0:T(8,128)(2,1)S(1)}, u32[]{:S(2)}, u32[]{:S(2)}) collective-permute-start(bf16[1,32,7168]{2,1,0:T(8,128)(2,1)S(1)} %copy-done.19), channel_id=1, source_target_pairs={{0,15},{1,14},{2,13},{3,12},{4,11},{5,10},{6,9},{7,8},{8,7},{9,6},... | collective-permute-start | bytes 1376264 | tf_op jit(solution)/shard_map/ppermute | solution.py:28
  273.5 121.0 %all-to-all-start.2 = ((bf16[16,32,7168]{2,1,0:T(8,128)(2,1)}), bf16[16,32,7168]{2,1,0:T(8,128)(2,1)}, u32[]{:S(2)}, u32[]{:S(2)}) async-start(bf16[16,32,7168]{2,1,0:T(8,128)(2,1)} %bitcast.208), calls=%async_computation.2 | async-start | bytes 14680064 | tf_op jit(solution)/shard_map/all_to_all | solution.py:134
  289.6 200.2 %collective-permute-start.17 = (bf16[128,7168]{1,0:T(8,128)(2,1)}, bf16[128,7168]{1,0:T(8,128)(2,1)}, u32[]{:S(2)}, u32[]{:S(2)}) collective-permute-start(bf16[128,7168]{1,0:T(8,128)(2,1)} %convolution_convert_fusion.4), channel_id=1, source_target_pairs={{0,8},{8,0},{1,9},{9,1},{2,10},{10,2},{3,11},{11,3},{4,12},{12,4},... | collective-permute-start | bytes 5505032 | tf_op jit(solution)/shard_map/ppermute | solution.py:40
  304.3 190.4 %collective-permute-start.16 = (bf16[7168,128]{1,0:T(8,128)(2,1)}, bf16[7168,128]{1,0:T(8,128)(2,1)}, u32[]{:S(2)}, u32[]{:S(2)}) collective-permute-start(bf16[7168,128]{1,0:T(8,128)(2,1)} %convolution_convert_fusion.6), channel_id=1, source_target_pairs={{0,8},{8,0},{1,9},{9,1},{2,10},{10,2},{3,11},{11,3},{4,12},{12,4},... | collective-permute-start | bytes 5505032 | tf_op jit(solution)/shard_map/ppermute | solution.py:40
  304.4 194.1 %collective-permute-start.15 = (bf16[7168,128]{1,0:T(8,128)(2,1)S(1)}, bf16[7168,128]{1,0:T(8,128)(2,1)}, u32[]{:S(2)}, u32[]{:S(2)}) collective-permute-start(bf16[7168,128]{1,0:T(8,128)(2,1)S(1)} %convolution_convert_fusion.8), channel_id=1, source_target_pairs={{0,8},{8,0},{1,9},{9,1},{2,10},{10,2},{3,11},{11,3},{4,12},{12,4},... | collective-permute-start | bytes 5505032 | tf_op jit(solution)/shard_map/ppermute | solution.py:40
  394.5 204.2 %all-to-all-start = ((bf16[16,32,7168]{2,1,0:T(8,128)(2,1)}), bf16[16,32,7168]{2,1,0:T(8,128)(2,1)}, u32[]{:S(2)}, u32[]{:S(2)}) async-start(bf16[16,32,7168]{2,1,0:T(8,128)(2,1)} %bitcast.207), calls=%async_computation | async-start | bytes 14680064 | tf_op jit(solution)/shard_map/all_to_all | solution.py:133
  489.6 138.3 %reduce-scatter.9.cloned.1.call-start = ((), (), s32[]{:S(2)}) async-start(), calls=%async_computation.6 | async-start | bytes 2064384
  507.9 134.6 %reduce-scatter.7.cloned.1.call-start = ((), (), s32[]{:S(2)}) async-start(), calls=%async_computation.5 | async-start | bytes 2064384
  608.6 35.6 %copy-start.1 = (bf16[32,7168]{1,0:T(8,128)(2,1)S(1)}, bf16[32,7168]{1,0:T(8,128)(2,1)}, u32[]{:S(2)}) copy-start(bf16[32,7168]{1,0:T(8,128)(2,1)} %param.8) | copy-start | bytes 1376260
  (18 other events, 72.7 us)
Sparse Core Ops, SparseCore 0:
  508.0 39.7 reduce-scatter.8
  608.5 33.9 reduce-scatter.6
